TPU v7x, 32 devices: a whole 2x2x4 slice. The times are simulated.
32 devices in a mesh: dom: 16 (over z, y, core), feat: 2 (over x).
Axes of the slice: x: 2, y: 2, z: 4, core: 2. Of those that a mesh axis runs over, the one named last changes fastest.
Arguments:
- node_features: bfloat16 [16384, 128], P('dom'), may hold values from -6 to 6
- weight: bfloat16 [128, 256], P(None, 'feat'), may hold values from -0.5 to 0.5
- bias: float32 [256], P('feat'), may hold values from -3 to 3
- tile_values: bfloat16 [1536, 128, 128], P('dom')
- tile_src: int32 [1536], P('dom'), may hold values from 0 to 7
- tile_dst: int32 [1536], P('dom'), may hold values from 0 to 31, as said below
- tile_counts: int32 [16], P('dom'), may hold values from 4 to 96
- out_grad: bfloat16 [16384, 256], P('dom', 'feat'), may hold values from -6 to 6
Outputs:
- output: bfloat16 [16384, 256], P('dom', 'feat')
- weight_grad: float32 [128, 256], P(None, 'feat')
- bias_grad: float32 [256], P('feat')
- input_grad: bfloat16 [16384, 128], P('dom', 'feat')
Inputs may be any that keep to these rules, and one draw needn't show every extreme that they name: The partition offset tile_dst[k] // 8 of slot k of a partition equals k mod 4.
All inputs are finite; a program needn't handle non-finite values.
Results may differ from a plain program's by a relative error of at most 0.0075.
Values may be sent and summed in bfloat16 or wider, within the bound.
No kernel may reach another device: no remote copies, remote signals or barrier semaphores. Data moves between devices by JAX's collectives and lax.ppermute only.
A program may use at most 64 MiB of HBM per device.

v0:
```python
import functools

import jax
import jax.numpy as jnp
from jax import lax
from jax.experimental import pallas as pl
from jax.experimental.pallas import tpu as pltpu
from jax.sharding import PartitionSpec as P

BLOCK = 128
REACH = 4
SUM_FLOPS = 10**9
SRC_UNIT = 2**16
F32 = jnp.float32
BF16 = jnp.bfloat16
VMEM = pl.BlockSpec(memory_space=pltpu.VMEM)
SMEM = pl.BlockSpec(memory_space=pltpu.SMEM)
HBM = pl.BlockSpec(memory_space=pltpu.HBM)


def call(kernel, out_shape, in_specs, out_specs, scratch=(), flops=0):
    return pl.pallas_call(
        kernel,
        out_shape=out_shape,
        in_specs=in_specs,
        out_specs=out_specs,
        scratch_shapes=list(scratch),
        compiler_params=pltpu.CompilerParams(vmem_limit_bytes=24 * 1024 * 1024),
        cost_estimate=pl.CostEstimate(flops=flops, bytes_accessed=2**20, transcendentals=0),
    )


def groups_at_once(groups):
    return next(m for m in (4, 3, 2, 1) if groups % m == 0)


def in_hbm(a):
    return pltpu.with_memory_space_constraint(a, pltpu.HBM)


def own_core():
    return lax.rem(lax.axis_index("dom"), 2)


def slot_loop(count, groups, offsets, body):
    m = groups_at_once(groups)
    pair = 2 if m % 2 == 0 else 1

    def chunk(i, carry):
        @pl.when(i * (m * REACH) < count)
        def _():
            for u in range(0, m, pair):
                for o in offsets:
                    body([i * m + u + v for v in range(pair)], o)

        return carry

    lax.fori_loop(0, groups // m, chunk, 0)


def side_by_side(lefts, tiles, contract):
    if len(tiles) == 1:
        left, right = lefts[0], tiles[0]
    else:
        left = jnp.concatenate(lefts, axis=1)
        none = jnp.zeros_like(tiles[0])
        right = jnp.concatenate(
            [jnp.concatenate([tiles[0], none], axis=1), jnp.concatenate([none, tiles[1]], axis=1)], axis=0
        )
    out = lax.dot_general(left, right, (((1,), (contract,)), ((), ())), preferred_element_type=F32)
    return [out[:, i * BLOCK : (i + 1) * BLOCK] for i in range(len(tiles))]


def source(entry):
    return lax.shift_right_logical(entry, 16)


def target(entry, o, blocks):
    return lax.bitwise_and(entry, SRC_UNIT - 1) - o * blocks


def push(xt, tiles, index, count, acc, js, o):
    blocks = xt.shape[0]
    ks = [j * REACH + o for j in js]
    outs = side_by_side([xt[source(index[k])] for k in ks], [tiles[j, o] for j in js], 1)
    for k, out in zip(ks, outs):
        acc[jnp.where(k < count, target(index[k], o, blocks), blocks)] += out


def pull(block, tiles, index, count, acc, js, o):
    blocks = acc.shape[0] - 1
    ks = [j * REACH + o for j in js]
    outs = side_by_side([block(target(index[k], o, blocks)) for k in ks], [tiles[j, o] for j in js], 0)
    for k, out in zip(ks, outs):
        acc[jnp.where(k < count, source(index[k]), blocks)] += out


def forward_swap_kernel(
    count, src_hbm, dst_hbm, x_hbm, tiles_hbm, tiles, xt, swap, index, src, dst, x, acc, small, large
):
    blocks, width, _ = xt.shape
    groups = tiles.shape[0]
    slots = src_hbm.shape[0]
    copies = [
        pltpu.make_async_copy(a, b, small.at[i])
        for i, (a, b) in enumerate(((x_hbm, x), (src_hbm, src), (dst_hbm, dst)))
    ]
    o = 3 - 2 * own_core()
    loads = [
        pltpu.make_async_copy(tiles_hbm.at[:, p], tiles.at[:, p], large.at[i])
        for i, p in enumerate((o, 2, 4 - o, 0))
    ]
    for c in copies + loads:
        c.start()
    acc[...] = jnp.zeros_like(acc)
    row = lax.broadcasted_iota(jnp.int32, (width, x.shape[1]), 0)
    column = lax.broadcasted_iota(jnp.int32, (width, x.shape[1]), 1)
    pick = (column == row + lax.axis_index("feat") * width).astype(BF16)
    for c in copies:
        c.wait()
    for b in range(blocks):
        xt[b] = lax.dot_general(
            pick, x[b * BLOCK : (b + 1) * BLOCK, :], (((1,), (1,)), ((), ())), preferred_element_type=F32
        ).astype(BF16)
    for k in range(slots):
        index[k] = src[k] * SRC_UNIT + dst[k]
    loads[0].wait()
    slot_loop(count[0], groups, (o,), functools.partial(push, xt, tiles, index, count[0], acc))
    swap[...] = acc[:blocks].astype(BF16)
    for c in loads[1:]:
        c.wait()


def forward_send_kernel(count, index, xt, tiles, acc2, direct, acc):
    acc2[...] = jnp.zeros_like(acc2)
    acc[...] = jnp.zeros_like(acc)
    far = 1 + 2 * own_core()

    def body(js, o):
        push(xt, tiles, index, count[0], acc2 if isinstance(o, int) else acc, js, o)

    slot_loop(count[0], tiles.shape[0], (2, far), body)
    direct[...] = acc[: direct.shape[0]].astype(BF16)


def forward_own_kernel(count, index, xt, tiles, acc):
    acc[...] = jnp.zeros_like(acc)
    slot_loop(count[0], tiles.shape[0], (0,), functools.partial(push, xt, tiles, index, count[0], acc))


def sum_kernel(n, first, *refs):
    for out in refs[n:]:
        blocks = out.shape[0]
        total = None
        for r in refs[:n]:
            part = r[...] if r.shape[0] == blocks else r[first : first + blocks]
            total = part.astype(F32) if total is None else total + part.astype(F32)
        out[...] = total.astype(out.dtype)
        first += blocks


def join_kernel(parts, *refs):
    out = refs[-1]
    halves = [refs[i : i + parts] for i in range(0, len(refs) - 1, parts)]
    first = 0
    for half in halves:
        blocks = half[0].shape[0]
        total = half[0][...].astype(F32)
        for r in half[1:]:
            total = total + r[...].astype(F32)
        out[first : first + blocks] = total.astype(out.dtype)
        first += blocks


def middle_kernel(parts, first, bias_ref, w_ref, og_ref, *refs):
    h_refs, (act, ht, grads), g_refs = refs[:parts], refs[parts : parts + 3], refs[parts + 3 :]
    blocks, width, _ = h_refs[0].shape
    f_in = w_ref.shape[0]
    me = lax.axis_index("feat")
    for q in range(parts):
        row = pl.multiple_of(lax.rem(me + q, parts) * width, width)
        for b in range(blocks):
            ht[pl.ds(row, width), b * BLOCK : (b + 1) * BLOCK] = h_refs[q][b]
    ht[f_in:, :] = jnp.ones((ht.shape[0] - f_in, ht.shape[1]), BF16)
    for b in range(blocks):
        rows = slice(b * BLOCK, (b + 1) * BLOCK)
        pre = lax.dot_general(
            ht[:f_in, rows], w_ref[...], (((0,), (0,)), ((), ())), preferred_element_type=F32
        ) + bias_ref[...]
        s = jax.nn.sigmoid(pre)
        act[rows, :] = (pre * s).astype(BF16)
        og = og_ref[(first + b) * BLOCK : (first + b + 1) * BLOCK, :].astype(F32)
        grad = (og * s * (1.0 + pre * (1.0 - s))).astype(BF16)
        grads[rows, :] = grad
        for q in range(parts):
            row = pl.multiple_of(lax.rem(me + q, parts) * width, width)
            g_refs[q][b] = lax.dot_general(
                w_ref[pl.ds(row, width), :], grad, (((1,), (1,)), ((), ())), preferred_element_type=F32
            ).astype(g_refs[q].dtype)


def weight_grad_kernel(n, *refs):
    hts, grads, (mine, other) = refs[:n], refs[n : 2 * n], refs[2 * n :]
    full = sum(jnp.dot(h[...], g[...], preferred_element_type=F32) for h, g in zip(hts, grads))
    full = full.astype(BF16)
    rows = mine.shape[0]
    low, high = full[:rows], full[rows:]
    first = own_core() == 0
    mine[...] = jnp.where(first, low, high)
    other[...] = jnp.where(first, high, low)


def swap_payload_kernel(g, *refs):
    parts, out = refs[:-1], refs[-1]
    blocks, width, _ = g.shape
    for b in range(blocks):
        out[b * width : (b + 1) * width, :] = g[b]
    total = paired_sum([r[...] for r in parts]).astype(BF16)
    rows, hid = total.shape
    if hid < out.shape[1]:
        out[blocks * width :, :] = jnp.zeros((rows, out.shape[1]), BF16)
    out[blocks * width :, :hid] = total


def backward_own_kernel(count, index, tiles, g, *refs):
    acts, (acc, out, sems) = refs[:-3], refs[-3:]
    copies, first = [], 0
    for i, act in enumerate(acts):
        rows = act.shape[0]
        copies.append(pltpu.make_async_copy(act, out.at[pl.ds(first, rows)], sems.at[i]))
        copies[-1].start()
        first += rows
    acc[...] = jnp.zeros_like(acc)
    slot_loop(
        count[0], tiles.shape[0], (0,), functools.partial(pull, lambda d: g[d], tiles, index, count[0], acc)
    )
    for c in copies:
        c.wait()


def backward_near_kernel(count, index, tiles, g2, gd, acc2, accd):
    acc2[...] = jnp.zeros_like(acc2)
    accd[...] = jnp.zeros_like(accd)
    far = 1 + 2 * own_core()

    def body(js, o):
        if isinstance(o, int):
            pull(lambda d: g2[d], tiles, index, count[0], acc2, js, o)
        else:
            pull(lambda d: gd[d], tiles, index, count[0], accd, js, o)

    slot_loop(count[0], tiles.shape[0], (2, far), body)


def backward_last_kernel(count, index, tiles, sent, got, acc0, acc2, accd, out, wg, bias, acc):
    blocks, width = acc.shape[0] - 1, acc.shape[1]
    f_in, hid = wg.shape
    acc[...] = jnp.zeros_like(acc)
    core = own_core()
    far = 3 - 2 * core

    def block(d):
        return got[pl.ds(pl.multiple_of(d * width, width), width), :]

    slot_loop(count[0], tiles.shape[0], (far,), functools.partial(pull, block, tiles, index, count[0], acc))
    for b in range(blocks):
        total = acc[b] + acc0[b] + acc2[b] + accd[b]
        out[:, b * BLOCK : (b + 1) * BLOCK] = total.astype(BF16)
    a, b = (r[blocks * width :, :hid].astype(F32) for r in (sent, got))
    low, high = jnp.where(core == 0, a, b), jnp.where(core == 0, b, a)
    rows = low.shape[0]
    wg[:rows, :] = low
    wg[rows:, :] = high[: f_in - rows]
    bias[...] = high[f_in - rows : f_in - rows + 1]


def paired_sum(parts):
    parts = [p.astype(F32) for p in parts]
    while len(parts) > 1:
        parts = [parts[i] + parts[i + 1] for i in range(0, len(parts), 2)]
    return parts[0]


def paired_sum_kernel(*refs):
    refs[-1][...] = paired_sum([r[...] for r in refs[:-1]]).astype(refs[-1].dtype)


def moved(block, axis, target):
    n = lax.axis_size(axis)
    return lax.ppermute(block, axis, [(i, target(i) % n) for i in range(n)])


def radices(n):
    out = []
    while n > 1:
        r = 4 if n % 4 == 0 else 2
        out.append(r)
        n //= r
    return out


def exchanged(part, axis, stride, r):
    return [part] + [moved(part, axis, lambda i, s=s: i ^ (s * stride)) for s in range(1, r)]


def shards(node_features, weight, bias, tile_values, tile_src, tile_dst, tile_counts, out_grad):
    nodes, f_in = node_features.shape
    hid = weight.shape[1]
    blocks = nodes // BLOCK
    parts = lax.axis_size("feat")
    width = f_in // parts
    capacity = tile_values.shape[0]
    groups = capacity // REACH
    piece = jax.ShapeDtypeStruct((blocks, width, BLOCK), BF16)
    totals = jax.ShapeDtypeStruct((blocks + 1, width, BLOCK), F32)
    acc = pltpu.VMEM(totals.shape, F32)
    tiles = jax.ShapeDtypeStruct((groups, REACH, BLOCK, BLOCK), BF16)
    slots = jax.ShapeDtypeStruct((capacity,), jnp.int32)
    rows = jax.ShapeDtypeStruct((nodes, hid), BF16)
    gradient = jax.ShapeDtypeStruct(((f_in + 32) // 2, hid), BF16)
    flops = 2 * capacity * BLOCK * BLOCK * width // REACH

    def swapped(i):
        return i ^ 1

    tiles, xt, swap, index = call(
        forward_swap_kernel,
        [tiles, piece, piece, slots],
        [SMEM] + [HBM] * 4,
        [VMEM] * 3 + [SMEM],
        [
            pltpu.SMEM((capacity,), jnp.int32),
            pltpu.SMEM((capacity,), jnp.int32),
            pltpu.VMEM(node_features.shape, BF16),
            acc,
            pltpu.SemaphoreType.DMA((3,)),
            pltpu.SemaphoreType.DMA((REACH,)),
        ],
        flops,
    )(tile_counts, *(in_hbm(a) for a in (tile_src, tile_dst, node_features, tile_values.reshape(tiles.shape))))
    index = (tile_counts, index)
    swap = moved(swap, "dom", swapped)
    acc2, direct = call(
        forward_send_kernel, [totals, piece], [SMEM] * 2 + [VMEM] * 2, [VMEM] * 2, [acc], 2 * flops
    )(*index, xt, tiles)
    cut = 2 if blocks % 2 == 0 else 1
    starts = range(0, blocks, blocks // cut)
    half = jax.ShapeDtypeStruct((blocks // cut, width, BLOCK), BF16)
    half_wide = jax.ShapeDtypeStruct(half.shape, F32)
    half_rows = jax.ShapeDtypeStruct((nodes // cut, hid), BF16)
    half_columns = jax.ShapeDtypeStruct((f_in + 32, nodes // cut), BF16)
    chip = call(functools.partial(sum_kernel, 2, 0), [half] * cut, [VMEM] * 2, [VMEM] * cut)(acc2, swap)
    chip = [moved(c, "dom", lambda i: i + 2) for c in chip]
    direct = moved(direct, "dom", lambda i: i + 1 + 2 * (i % 2))
    (acc0,) = call(forward_own_kernel, [totals], [SMEM] * 2 + [VMEM] * 2, [VMEM], (), flops)(*index, xt, tiles)
    h_lists = []
    for first, c in zip(starts, chip):
        (h,) = call(functools.partial(sum_kernel, 3, first), [half], [VMEM] * 3, [VMEM])(acc0, direct, c)
        h_lists.append([h] + [moved(h, "feat", lambda i, q=q: i - q) for q in range(1, parts)])
    acts, hts, grads, g_list = [], [], [], []
    for first, hs in zip(starts, h_lists):
        act, ht, grad, g_own, *g_others = call(
            functools.partial(middle_kernel, parts, first),
            [half_rows, half_columns, half_rows, half_wide] + [half] * (parts - 1),
            [VMEM] * (3 + parts),
            [VMEM] * (3 + parts),
            (),
            4 * nodes * f_in * hid // cut,
        )(bias.reshape(1, hid), weight, out_grad, *hs)
        acts.append(act)
        hts.append(ht)
        grads.append(grad)
        g_list += [g_own] + [moved(g, "feat", lambda i, q=q + 1: i + q) for q, g in enumerate(g_others)]
    wg, wg_other = call(
        functools.partial(weight_grad_kernel, cut),
        [gradient, gradient],
        [VMEM] * (2 * cut),
        [VMEM, VMEM],
        (),
        2 * nodes * f_in * hid,
    )(*hts, *grads)
    r, *more = radices(lax.axis_size("dom"))
    wgs = [wg] + [moved(wg_other if s % 2 else wg, "dom", lambda i, s=s: i ^ s) for s in range(1, r)]
    (g,) = call(functools.partial(join_kernel, parts), [piece], [VMEM] * len(g_list), [VMEM])(*g_list)
    g_chip = moved(g, "dom", lambda i: i - 2)
    g_direct = moved(g, "dom", lambda i: i - 3 + 2 * (i % 2))
    stride = r
    for r in more:
        (wg,) = call(paired_sum_kernel, [gradient], [VMEM] * len(wgs), [VMEM], (), SUM_FLOPS)(*wgs)
        wgs = exchanged(wg, "dom", stride, r)
        stride *= r
    back0, output = call(
        backward_own_kernel,
        [totals, rows],
        [SMEM] * 2 + [VMEM] * (2 + cut),
        [VMEM, HBM],
        [pltpu.SemaphoreType.DMA((cut,))],
        flops,
    )(*index, tiles, g, *acts)
    back0, g_chip, g_direct, *wgs = lax.optimization_barrier((back0, g_chip, g_direct, *wgs))
    payload = jax.ShapeDtypeStruct((blocks * width + gradient.shape[0], BLOCK), BF16)
    (sent,) = call(swap_payload_kernel, [payload], [VMEM] * (1 + len(wgs)), [VMEM])(g_chip, *wgs)
    got = moved(sent, "dom", swapped)
    back2, backd = call(
        backward_near_kernel, [totals, totals], [SMEM] * 2 + [VMEM] * 3, [VMEM] * 2, (), 2 * flops
    )(*index, tiles, g_chip, g_direct)
    input_grad, weight_grad, bias_grad = call(
        backward_last_kernel,
        [
            jax.ShapeDtypeStruct((width, nodes), BF16),
            jax.ShapeDtypeStruct((f_in, hid), F32),
            jax.ShapeDtypeStruct((1, hid), F32),
        ],
        [SMEM] * 2 + [VMEM] * 6,
        [VMEM] * 3,
        [acc],
        flops,
    )(*index, tiles, sent, got, back0, back2, backd)
    return output, weight_grad, bias_grad.reshape(hid), input_grad.T


def solution(mesh):
    return jax.shard_map(
        shards,
        mesh=mesh,
        in_specs=(
            P("dom", None),
            P(None, "feat"),
            P("feat"),
            P("dom", None, None),
            P("dom"),
            P("dom"),
            P("dom"),
            P("dom", "feat"),
        ),
        out_specs=(P("dom", "feat"), P(None, "feat"), P("feat"), P("dom", "feat")),
        check_vma=False,
    )
```

profile of v0, /device:TPU:5, one launch (start us, length us, event | category | flops | bytes accessed | tf_op | source)
XLA Modules:
  0.0 40.3 jit_solution(13797511508071617801)
XLA Ops:
  1.3 3.3 %shard_map.111 = (bf16[24,4,128,128]{3,2,1,0:T(8,128)(2,1)S(1)}, bf16[8,64,128]{2,1,0:T(8,128)(2,1)S(1)}, bf16[8,64,128]{2,1,0:T(8,128)(2,1)S(1)}, s32[96]{0:T(128)S(1)}) custom-call(s32[1]{0:T(128)S(6)} %copy.12.count, s32[96]{0:T(128)} %src_hbm.1, s32[96]{0:T(128)} %dst_hbm.1, bf16[1024,128]{1,0:T(8,128)(2,1)} %x_hbm.1, bf16[24,4,128,128]{3,2,1,0:T(8,128)(2,1)} %bitcast.6), custom_call_target="tpu_custom_call" | custom-call | flops 50331648 | bytes 1048576 | tf_op jit(solution)/shard_map/pallas_call | solution.py:326
  4.6 2.4 %shard_map.113 = (f32[9,64,128]{2,1,0:T(8,128)S(1)}, bf16[8,64,128]{2,1,0:T(8,128)(2,1)S(1)}) custom-call(s32[1]{0:T(128)S(6)} %copy.12.count, s32[96]{0:T(128)S(1)} %get-tuple-element.38.index, bf16[8,64,128]{2,1,0:T(8,128)(2,1)S(1)} %get-tuple-element.40.xt, bf16[24,4,128,128]{3,2,1,0:T(8,128)(2,1)S(1)} %get-tuple-element.39.tiles), custom_call_target="tpu_custom_call" | custom-call | flops 100663296 | bytes 1048576 | tf_op jit(solution)/shard_map/pallas_call | solution.py:343
  7.2 1.3 %collective-permute-start.5 = (bf16[4,64,128]{2,1,0:T(8,128)(2,1)S(1)}, bf16[4,64,128]{2,1,0:T(8,128)(2,1)S(1)}, u32[]{:S(2)}, u32[]{:S(2)}) collective-permute-start(bf16[4,64,128]{2,1,0:T(8,128)(2,1)S(1)} %get-tuple-element.47), channel_id=1, source_target_pairs={{0,4},{2,6},{4,8},{6,10},{8,12},{10,14},{12,16},{14,18},{16,20},{1... | collective-permute-start | bytes 196616 | tf_op jit(solution)/shard_map/ppermute | solution.py:290
  8.5 1.2 %collective-permute-start.2 = (bf16[4,64,128]{2,1,0:T(8,128)(2,1)S(1)}, bf16[4,64,128]{2,1,0:T(8,128)(2,1)S(1)}, u32[]{:S(2)}, u32[]{:S(2)}) collective-permute-start(bf16[4,64,128]{2,1,0:T(8,128)(2,1)S(1)} %get-tuple-element.44), channel_id=1, source_target_pairs={{0,4},{2,6},{4,8},{6,10},{8,12},{10,14},{12,16},{14,18},{16,20},{1... | collective-permute-start | bytes 196616 | tf_op jit(solution)/shard_map/ppermute | solution.py:290
  9.7 1.9 %shard_map.112.refs_0_ = f32[9,64,128]{2,1,0:T(8,128)S(1)} custom-call(s32[1]{0:T(128)S(6)} %copy.12.count, s32[96]{0:T(128)S(1)} %get-tuple-element.38.index, bf16[8,64,128]{2,1,0:T(8,128)(2,1)S(1)} %get-tuple-element.40.xt, bf16[24,4,128,128]{3,2,1,0:T(8,128)(2,1)S(1)} %get-tuple-element.39.tiles), custom_call_target="tpu_custom_call" | custom-call | flops 50331648 | bytes 1048576 | tf_op jit(solution)/shard_map/pallas_call | solution.py:355
  11.7 1.3 %collective-permute-start.6 = (bf16[4,64,128]{2,1,0:T(8,128)(2,1)S(1)}, bf16[4,64,128]{2,1,0:T(8,128)(2,1)S(1)}, u32[]{:S(2)}, u32[]{:S(2)}) collective-permute-start(bf16[4,64,128]{2,1,0:T(8,128)(2,1)S(1)} %shard_map.117.refs_0_), channel_id=1, source_target_pairs={{0,1},{1,0},{2,3},{3,2},{4,5},{5,4},{6,7},{7,6},{8,9},{9,8},{10,11... | collective-permute-start | bytes 196616 | tf_op jit(solution)/shard_map/ppermute | solution.py:290
  13.0 0.9 %collective-permute-start.3 = (bf16[4,64,128]{2,1,0:T(8,128)(2,1)S(1)}, bf16[4,64,128]{2,1,0:T(8,128)(2,1)S(1)}, u32[]{:S(2)}, u32[]{:S(2)}) collective-permute-start(bf16[4,64,128]{2,1,0:T(8,128)(2,1)S(1)} %shard_map.115.refs_0_), channel_id=1, source_target_pairs={{0,1},{1,0},{2,3},{3,2},{4,5},{5,4},{6,7},{7,6},{8,9},{9,8},{10,11... | collective-permute-start | bytes 196616 | tf_op jit(solution)/shard_map/ppermute | solution.py:290
  13.9 1.0 %collective-permute-done.6.refs_1_ = bf16[4,64,128]{2,1,0:T(8,128)(2,1)S(1)} collective-permute-done((bf16[4,64,128]{2,1,0:T(8,128)(2,1)S(1)}, bf16[4,64,128]{2,1,0:T(8,128)(2,1)S(1)}, u32[]{:S(2)}, u32[]{:S(2)}) %collective-permute-start.6) | collective-permute-done | bytes 65568 | tf_op jit(solution)/shard_map/ppermute | solution.py:290
  14.9 0.9 %shard_map.118 = (bf16[512,128]{1,0:T(8,128)(2,1)S(1)}, bf16[160,512]{1,0:T(8,128)(2,1)S(1)}, bf16[512,128]{1,0:T(8,128)(2,1)S(1)}, f32[4,64,128]{2,1,0:T(8,128)S(1)}, bf16[4,64,128]{2,1,0:T(8,128)(2,1)S(1)}) custom-call(f32[1,128]{1,0:T(1,128)S(1)} %bitcast.4, bf16[128,128]{1,0:T(8,128)(2,1)S(1)} %copy-done.1, bf16[1024,128]{1,0:T(8,128)(2,1)S(1)} %copy-done, ...), custom_call_target="tpu_custom_call" | custom-call | flops 33554432 | bytes 1048576 | tf_op jit(solution)/shard_map/pallas_call | solution.py:362
  15.8 1.2 %collective-permute-start.7 = (bf16[4,64,128]{2,1,0:T(8,128)(2,1)S(1)}, bf16[4,64,128]{2,1,0:T(8,128)(2,1)S(1)}, u32[]{:S(2)}, u32[]{:S(2)}) collective-permute-start(bf16[4,64,128]{2,1,0:T(8,128)(2,1)S(1)} %get-tuple-element.49), channel_id=1, source_target_pairs={{0,1},{1,0},{2,3},{3,2},{4,5},{5,4},{6,7},{7,6},{8,9},{9,8},{10,11... | collective-permute-start | bytes 196616 | tf_op jit(solution)/shard_map/ppermute | solution.py:290
  17.0 0.9 %shard_map.116 = (bf16[512,128]{1,0:T(8,128)(2,1)S(1)}, bf16[160,512]{1,0:T(8,128)(2,1)S(1)}, bf16[512,128]{1,0:T(8,128)(2,1)S(1)}, f32[4,64,128]{2,1,0:T(8,128)S(1)}, bf16[4,64,128]{2,1,0:T(8,128)(2,1)S(1)}) custom-call(f32[1,128]{1,0:T(1,128)S(1)} %bitcast.5, bf16[128,128]{1,0:T(8,128)(2,1)S(1)} %copy-done.1, bf16[1024,128]{1,0:T(8,128)(2,1)S(1)} %copy-done, ...), custom_call_target="tpu_custom_call" | custom-call | flops 33554432 | bytes 1048576 | tf_op jit(solution)/shard_map/pallas_call | solution.py:362
  17.9 0.3 collective-permute-start.4
  18.2 0.2 shard_map.121
  18.4 3.5 %collective-permute-start.10 = (bf16[80,128]{1,0:T(8,128)(2,1)S(1)}, bf16[80,128]{1,0:T(8,128)(2,1)S(1)}, u32[]{:S(2)}, u32[]{:S(2)}) collective-permute-start(bf16[80,128]{1,0:T(8,128)(2,1)S(1)} %get-tuple-element.59), channel_id=1, source_target_pairs={{0,2},{2,0},{4,6},{6,4},{8,10},{10,8},{12,14},{14,12},{16,18},{18,... | collective-permute-start | bytes 61448 | tf_op jit(solution)/shard_map/ppermute | solution.py:290
  21.9 1.9 %collective-permute-start.11 = (bf16[80,128]{1,0:T(8,128)(2,1)S(1)}, bf16[80,128]{1,0:T(8,128)(2,1)S(1)}, u32[]{:S(2)}, u32[]{:S(2)}) collective-permute-start(bf16[80,128]{1,0:T(8,128)(2,1)S(1)} %get-tuple-element.58.refs_0_), channel_id=1, source_target_pairs={{0,4},{2,6},{4,0},{6,2},{8,12},{10,14},{12,8},{14,10},{16,20},{18,... | collective-permute-start | bytes 61448 | tf_op jit(solution)/shard_map/ppermute | solution.py:290
  23.8 1.7 %collective-permute-start.8 = (bf16[8,64,128]{2,1,0:T(8,128)(2,1)S(1)}, bf16[8,64,128]{2,1,0:T(8,128)(2,1)S(1)}, u32[]{:S(2)}, u32[]{:S(2)}) collective-permute-start(bf16[8,64,128]{2,1,0:T(8,128)(2,1)S(1)} %shard_map.119.g), channel_id=1, source_target_pairs={{0,28},{2,30},{4,0},{6,2},{8,4},{10,6},{12,8},{14,10},{16,12},{18,... | collective-permute-start | bytes 393224 | tf_op jit(solution)/shard_map/ppermute | solution.py:290
  25.5 1.9 %collective-permute-start.9 = (bf16[8,64,128]{2,1,0:T(8,128)(2,1)S(1)}, bf16[8,64,128]{2,1,0:T(8,128)(2,1)S(1)}, u32[]{:S(2)}, u32[]{:S(2)}) collective-permute-start(bf16[8,64,128]{2,1,0:T(8,128)(2,1)S(1)} %shard_map.119.g), channel_id=1, source_target_pairs={{0,26},{2,0},{4,30},{6,4},{8,2},{10,8},{12,6},{14,12},{16,10},{18,... | collective-permute-start | bytes 393224 | tf_op jit(solution)/shard_map/ppermute | solution.py:290
  27.6 2.0 %collective-permute-start.14 = (bf16[80,128]{1,0:T(8,128)(2,1)S(1)}, bf16[80,128]{1,0:T(8,128)(2,1)S(1)}, u32[]{:S(2)}, u32[]{:S(2)}) collective-permute-start(bf16[80,128]{1,0:T(8,128)(2,1)S(1)} %shard_map.122.refs_0_), channel_id=1, source_target_pairs={{0,16},{2,18},{4,20},{6,22},{8,24},{10,26},{12,28},{14,30},{16,0},... | collective-permute-start | bytes 61448 | tf_op jit(solution)/shard_map/ppermute | solution.py:290
  29.6 1.5 %collective-permute-start.15 = (bf16[80,128]{1,0:T(8,128)(2,1)S(1)}, bf16[80,128]{1,0:T(8,128)(2,1)S(1)}, u32[]{:S(2)}, u32[]{:S(2)}) collective-permute-start(bf16[80,128]{1,0:T(8,128)(2,1)S(1)} %shard_map.122.refs_0_), channel_id=1, source_target_pairs={{0,24},{2,26},{4,28},{6,30},{8,16},{10,18},{12,20},{14,22},{16,8},... | collective-permute-start | bytes 61448 | tf_op jit(solution)/shard_map/ppermute | solution.py:290
  31.1 1.7 %shard_map.120 = (f32[9,64,128]{2,1,0:T(8,128)S(1)}, bf16[1024,128]{1,0:T(8,128)(2,1)}) custom-call(s32[1]{0:T(128)S(6)} %copy.12.count, s32[96]{0:T(128)S(1)} %get-tuple-element.38.index, bf16[24,4,128,128]{3,2,1,0:T(8,128)(2,1)S(1)} %get-tuple-element.39.tiles, bf16[8,64,128]{2,1,0:T(8,128)(2,1)S(1)} %shard_map.119.g, ...), custom_call_target="tpu_custom_call" | custom-call | flops 50331648 | bytes 1048576 | tf_op jit(solution)/shard_map/pallas_call | solution.py:392
  32.9 1.2 %collective-permute-done.15.refs_3_ = bf16[80,128]{1,0:T(8,128)(2,1)S(1)} collective-permute-done((bf16[80,128]{1,0:T(8,128)(2,1)S(1)}, bf16[80,128]{1,0:T(8,128)(2,1)S(1)}, u32[]{:S(2)}, u32[]{:S(2)}) %collective-permute-start.15) | collective-permute-done | bytes 20512 | tf_op jit(solution)/shard_map/ppermute | solution.py:290
  34.0 1.8 %collective-permute-start.16 = (bf16[592,128]{1,0:T(8,128)(2,1)S(1)}, bf16[592,128]{1,0:T(8,128)(2,1)S(1)}, u32[]{:S(2)}, u32[]{:S(2)}) collective-permute-start(bf16[592,128]{1,0:T(8,128)(2,1)S(1)} %shard_map.123.sent), channel_id=1, source_target_pairs={{0,2},{2,0},{4,6},{6,4},{8,10},{10,8},{12,14},{14,12},{16,18},{18,... | collective-permute-start | bytes 454664 | tf_op jit(solution)/shard_map/ppermute | solution.py:290
  35.8 2.0 %shard_map.124 = (f32[9,64,128]{2,1,0:T(8,128)S(1)}, f32[9,64,128]{2,1,0:T(8,128)S(1)}) custom-call(s32[1]{0:T(128)S(6)} %copy.12.count, s32[96]{0:T(128)S(1)} %get-tuple-element.38.index, bf16[24,4,128,128]{3,2,1,0:T(8,128)(2,1)S(1)} %get-tuple-element.39.tiles, bf16[8,64,128]{2,1,0:T(8,128)(2,1)S(1)} %collective-permute-done.8.g.g2, ...), custom_call_target="tpu_custom_call" | custom-call | flops 100663296 | bytes 1048576 | tf_op jit(solution)/shard_map/pallas_call | solution.py:404
  37.8 2.5 %shard_map.125 = (bf16[64,1024]{1,0:T(8,128)(2,1)}, f32[128,128]{1,0:T(8,128)}, f32[1,128]{1,0:T(1,128)}) custom-call(s32[1]{0:T(128)S(6)} %copy.12.count, s32[96]{0:T(128)S(1)} %get-tuple-element.38.index, bf16[24,4,128,128]{3,2,1,0:T(8,128)(2,1)S(1)} %get-tuple-element.39.tiles, bf16[592,128]{1,0:T(8,128)(2,1)S(1)} %shard_map.123.sent, ...), custom_call_target="tpu_custom_call" | custom-call | flops 50331648 | bytes 1048576 | tf_op jit(solution)/shard_map/pallas_call | solution.py:407
  (31 shorter events, 0.5 us)
Async XLA Ops:
  4.6 2.6 %collective-permute-start.1 = (bf16[8,64,128]{2,1,0:T(8,128)(2,1)S(1)}, bf16[8,64,128]{2,1,0:T(8,128)(2,1)S(1)}, u32[]{:S(2)}, u32[]{:S(2)}) collective-permute-start(bf16[8,64,128]{2,1,0:T(8,128)(2,1)S(1)} %get-tuple-element.43), channel_id=1, source_target_pairs={{0,2},{2,0},{4,6},{6,4},{8,10},{10,8},{12,14},{14,12},{16,18},{18,... | collective-permute-start | bytes 393224 | tf_op jit(solution)/shard_map/ppermute | solution.py:290
  7.0 7.9 %copy-start = (bf16[1024,128]{1,0:T(8,128)(2,1)S(1)}, bf16[1024,128]{1,0:T(8,128)(2,1)}, u32[]{:S(2)}) copy-start(bf16[1024,128]{1,0:T(8,128)(2,1)} %og_ref.3) | copy-start | bytes 786436
  7.0 7.8 %copy-start.1 = (bf16[128,128]{1,0:T(8,128)(2,1)S(1)}, bf16[128,128]{1,0:T(8,128)(2,1)}, u32[]{:S(2)}) copy-start(bf16[128,128]{1,0:T(8,128)(2,1)} %w_ref.3) | copy-start | bytes 98308
  7.1 7.8 %copy-start.2 = (f32[128]{0:T(128)S(1)}, f32[128]{0:T(128)}, u32[]{:S(2)}) copy-start(f32[128]{0:T(128)} %param.10) | copy-start | bytes 1540
  7.1 4.6 %collective-permute-start = (bf16[8,64,128]{2,1,0:T(8,128)(2,1)S(1)}, bf16[8,64,128]{2,1,0:T(8,128)(2,1)S(1)}, u32[]{:S(2)}, u32[]{:S(2)}) collective-permute-start(bf16[8,64,128]{2,1,0:T(8,128)(2,1)S(1)} %get-tuple-element.41), channel_id=1, source_target_pairs={{0,2},{2,8},{4,6},{6,12},{8,10},{10,16},{12,14},{14,20},{16,18},{1... | collective-permute-start | bytes 393224 | tf_op jit(solution)/shard_map/ppermute | solution.py:290
  7.2 4.5 %collective-permute-start.5 = (bf16[4,64,128]{2,1,0:T(8,128)(2,1)S(1)}, bf16[4,64,128]{2,1,0:T(8,128)(2,1)S(1)}, u32[]{:S(2)}, u32[]{:S(2)}) collective-permute-start(bf16[4,64,128]{2,1,0:T(8,128)(2,1)S(1)} %get-tuple-element.47), channel_id=1, source_target_pairs={{0,4},{2,6},{4,8},{6,10},{8,12},{10,14},{12,16},{14,18},{16,20},{1... | collective-permute-start | bytes 196616 | tf_op jit(solution)/shard_map/ppermute | solution.py:290
  8.5 4.5 %collective-permute-start.2 = (bf16[4,64,128]{2,1,0:T(8,128)(2,1)S(1)}, bf16[4,64,128]{2,1,0:T(8,128)(2,1)S(1)}, u32[]{:S(2)}, u32[]{:S(2)}) collective-permute-start(bf16[4,64,128]{2,1,0:T(8,128)(2,1)S(1)} %get-tuple-element.44), channel_id=1, source_target_pairs={{0,4},{2,6},{4,8},{6,10},{8,12},{10,14},{12,16},{14,18},{16,20},{1... | collective-permute-start | bytes 196616 | tf_op jit(solution)/shard_map/ppermute | solution.py:290
  11.7 3.2 %collective-permute-start.6 = (bf16[4,64,128]{2,1,0:T(8,128)(2,1)S(1)}, bf16[4,64,128]{2,1,0:T(8,128)(2,1)S(1)}, u32[]{:S(2)}, u32[]{:S(2)}) collective-permute-start(bf16[4,64,128]{2,1,0:T(8,128)(2,1)S(1)} %shard_map.117.refs_0_), channel_id=1, source_target_pairs={{0,1},{1,0},{2,3},{3,2},{4,5},{5,4},{6,7},{7,6},{8,9},{9,8},{10,11... | collective-permute-start | bytes 196616 | tf_op jit(solution)/shard_map/ppermute | solution.py:290
  13.0 4.0 %collective-permute-start.3 = (bf16[4,64,128]{2,1,0:T(8,128)(2,1)S(1)}, bf16[4,64,128]{2,1,0:T(8,128)(2,1)S(1)}, u32[]{:S(2)}, u32[]{:S(2)}) collective-permute-start(bf16[4,64,128]{2,1,0:T(8,128)(2,1)S(1)} %shard_map.115.refs_0_), channel_id=1, source_target_pairs={{0,1},{1,0},{2,3},{3,2},{4,5},{5,4},{6,7},{7,6},{8,9},{9,8},{10,11... | collective-permute-start | bytes 196616 | tf_op jit(solution)/shard_map/ppermute | solution.py:290
  15.8 8.0 %collective-permute-start.7 = (bf16[4,64,128]{2,1,0:T(8,128)(2,1)S(1)}, bf16[4,64,128]{2,1,0:T(8,128)(2,1)S(1)}, u32[]{:S(2)}, u32[]{:S(2)}) collective-permute-start(bf16[4,64,128]{2,1,0:T(8,128)(2,1)S(1)} %get-tuple-element.49), channel_id=1, source_target_pairs={{0,1},{1,0},{2,3},{3,2},{4,5},{5,4},{6,7},{7,6},{8,9},{9,8},{10,11... | collective-permute-start | bytes 196616 | tf_op jit(solution)/shard_map/ppermute | solution.py:290
  17.9 5.9 %collective-permute-start.4 = (bf16[4,64,128]{2,1,0:T(8,128)(2,1)S(1)}, bf16[4,64,128]{2,1,0:T(8,128)(2,1)S(1)}, u32[]{:S(2)}, u32[]{:S(2)}) collective-permute-start(bf16[4,64,128]{2,1,0:T(8,128)(2,1)S(1)} %get-tuple-element.46), channel_id=1, source_target_pairs={{0,1},{1,0},{2,3},{3,2},{4,5},{5,4},{6,7},{7,6},{8,9},{9,8},{10,11... | collective-permute-start | bytes 196616 | tf_op jit(solution)/shard_map/ppermute | solution.py:290
  18.4 9.0 %collective-permute-start.10 = (bf16[80,128]{1,0:T(8,128)(2,1)S(1)}, bf16[80,128]{1,0:T(8,128)(2,1)S(1)}, u32[]{:S(2)}, u32[]{:S(2)}) collective-permute-start(bf16[80,128]{1,0:T(8,128)(2,1)S(1)} %get-tuple-element.59), channel_id=1, source_target_pairs={{0,2},{2,0},{4,6},{6,4},{8,10},{10,8},{12,14},{14,12},{16,18},{18,... | collective-permute-start | bytes 61448 | tf_op jit(solution)/shard_map/ppermute | solution.py:290
  21.9 5.6 %collective-permute-start.11 = (bf16[80,128]{1,0:T(8,128)(2,1)S(1)}, bf16[80,128]{1,0:T(8,128)(2,1)S(1)}, u32[]{:S(2)}, u32[]{:S(2)}) collective-permute-start(bf16[80,128]{1,0:T(8,128)(2,1)S(1)} %get-tuple-element.58.refs_0_), channel_id=1, source_target_pairs={{0,4},{2,6},{4,0},{6,2},{8,12},{10,14},{12,8},{14,10},{16,20},{18,... | collective-permute-start | bytes 61448 | tf_op jit(solution)/shard_map/ppermute | solution.py:290
  23.8 3.7 %collective-permute-start.12 = (bf16[80,128]{1,0:T(8,128)(2,1)S(1)}, bf16[80,128]{1,0:T(8,128)(2,1)S(1)}, u32[]{:S(2)}, u32[]{:S(2)}) collective-permute-start(bf16[80,128]{1,0:T(8,128)(2,1)S(1)} %get-tuple-element.59), channel_id=1, source_target_pairs={{0,6},{2,4},{4,2},{6,0},{8,14},{10,12},{12,10},{14,8},{16,22},{18,... | collective-permute-start | bytes 61448 | tf_op jit(solution)/shard_map/ppermute | solution.py:290
  23.8 10.2 %collective-permute-start.8 = (bf16[8,64,128]{2,1,0:T(8,128)(2,1)S(1)}, bf16[8,64,128]{2,1,0:T(8,128)(2,1)S(1)}, u32[]{:S(2)}, u32[]{:S(2)}) collective-permute-start(bf16[8,64,128]{2,1,0:T(8,128)(2,1)S(1)} %shard_map.119.g), channel_id=1, source_target_pairs={{0,28},{2,30},{4,0},{6,2},{8,4},{10,6},{12,8},{14,10},{16,12},{18,... | collective-permute-start | bytes 393224 | tf_op jit(solution)/shard_map/ppermute | solution.py:290
  25.5 8.5 %collective-permute-start.9 = (bf16[8,64,128]{2,1,0:T(8,128)(2,1)S(1)}, bf16[8,64,128]{2,1,0:T(8,128)(2,1)S(1)}, u32[]{:S(2)}, u32[]{:S(2)}) collective-permute-start(bf16[8,64,128]{2,1,0:T(8,128)(2,1)S(1)} %shard_map.119.g), channel_id=1, source_target_pairs={{0,26},{2,0},{4,30},{6,4},{8,2},{10,8},{12,6},{14,12},{16,10},{18,... | collective-permute-start | bytes 393224 | tf_op jit(solution)/shard_map/ppermute | solution.py:290
  27.5 5.3 %collective-permute-start.13 = (bf16[80,128]{1,0:T(8,128)(2,1)S(1)}, bf16[80,128]{1,0:T(8,128)(2,1)S(1)}, u32[]{:S(2)}, u32[]{:S(2)}) collective-permute-start(bf16[80,128]{1,0:T(8,128)(2,1)S(1)} %shard_map.122.refs_0_), channel_id=1, source_target_pairs={{0,8},{2,10},{4,12},{6,14},{8,0},{10,2},{12,4},{14,6},{16,24},{18,... | collective-permute-start | bytes 61448 | tf_op jit(solution)/shard_map/ppermute | solution.py:290
  27.6 5.3 %collective-permute-start.14 = (bf16[80,128]{1,0:T(8,128)(2,1)S(1)}, bf16[80,128]{1,0:T(8,128)(2,1)S(1)}, u32[]{:S(2)}, u32[]{:S(2)}) collective-permute-start(bf16[80,128]{1,0:T(8,128)(2,1)S(1)} %shard_map.122.refs_0_), channel_id=1, source_target_pairs={{0,16},{2,18},{4,20},{6,22},{8,24},{10,26},{12,28},{14,30},{16,0},... | collective-permute-start | bytes 61448 | tf_op jit(solution)/shard_map/ppermute | solution.py:290
  29.6 4.4 %collective-permute-start.15 = (bf16[80,128]{1,0:T(8,128)(2,1)S(1)}, bf16[80,128]{1,0:T(8,128)(2,1)S(1)}, u32[]{:S(2)}, u32[]{:S(2)}) collective-permute-start(bf16[80,128]{1,0:T(8,128)(2,1)S(1)} %shard_map.122.refs_0_), channel_id=1, source_target_pairs={{0,24},{2,26},{4,28},{6,30},{8,16},{10,18},{12,20},{14,22},{16,8},... | collective-permute-start | bytes 61448 | tf_op jit(solution)/shard_map/ppermute | solution.py:290
  34.0 3.8 %collective-permute-start.16 = (bf16[592,128]{1,0:T(8,128)(2,1)S(1)}, bf16[592,128]{1,0:T(8,128)(2,1)S(1)}, u32[]{:S(2)}, u32[]{:S(2)}) collective-permute-start(bf16[592,128]{1,0:T(8,128)(2,1)S(1)} %shard_map.123.sent), channel_id=1, source_target_pairs={{0,2},{2,0},{4,6},{6,4},{8,10},{10,8},{12,14},{14,12},{16,18},{18,... | collective-permute-start | bytes 454664 | tf_op jit(solution)/shard_map/ppermute | solution.py:290
where the time goes:
time: 40.4 us; the launch traced here: 40.3 us
  starting transfers between devices  20.8 us (51%)
  Pallas kernels  15.9 us (39%)
  waiting for transfers between devices  2.16 us (5%)
  between operations  1.46 us (4%)
    ppermute x17, starting transfers between devices, moved(): return lax.ppermute(block, axis, [(i, target(i) % n) for i in range(n)])  20.8 us
    pallas_call x1, Pallas kernels, shards(): call(forward_swap_kernel, [tiles, piece, piece, slots], [SMEM] + [HBM] *...  3.26 us
    pallas_call x1, Pallas kernels, shards(): call(backward_last_kernel, [jax.ShapeDtypeStruct((width, nodes), BF16), j...  2.49 us
    pallas_call x1, Pallas kernels, shards(): call(forward_send_kernel, [totals, piece], [SMEM] * 2 + [VMEM] * 2, [VMEM...  2.39 us
    ppermute x17, waiting for transfers between devices, moved(): return lax.ppermute(block, axis, [(i, target(i) % n) for i in range(n)])  2.16 us
    pallas_call x1, Pallas kernels, shards(): call(backward_near_kernel, [totals, totals], [SMEM] * 2 + [VMEM] * 3, [VM...  1.98 us
    pallas_call x1, Pallas kernels, shards(): call(forward_own_kernel, [totals], [SMEM] * 2 + [VMEM] * 2, [VMEM], (), f...  1.9 us
    pallas_call x2, Pallas kernels, shards(): call(functools.partial(middle_kernel, parts, first), [half_rows, half_col...  1.8 us
  transfers between devices with their start and end apart: 17, of which 2 were waited for; matrix products, arithmetic and copies ran while one was open for 0% of the time, Pallas kernels for 25%

commit v1 on v0

--- a/solution.py
+++ b/solution.py
@@ -82,7 +82,8 @@
 def push(xt, tiles, index, count, acc, js, o):
     blocks = xt.shape[0]
     ks = [j * REACH + o for j in js]
-    outs = side_by_side([xt[source(index[k])] for k in ks], [tiles[j, o] for j in js], 1)
+    plane = o if tiles.shape[1] == REACH else 0
+    outs = side_by_side([xt[source(index[k])] for k in ks], [tiles[j, plane] for j in js], 1)
     for k, out in zip(ks, outs):
         acc[jnp.where(k < count, target(index[k], o, blocks), blocks)] += out
 
@@ -96,21 +97,17 @@
 
 
 def forward_swap_kernel(
-    count, src_hbm, dst_hbm, x_hbm, tiles_hbm, tiles, xt, swap, index, src, dst, x, acc, small, large
+    count, src_hbm, dst_hbm, x_hbm, tiles_hbm, xt, swap, index, src, dst, x, tiles, acc, sems
 ):
     blocks, width, _ = xt.shape
-    groups = tiles.shape[0]
+    groups = tiles_hbm.shape[0]
     slots = src_hbm.shape[0]
-    copies = [
-        pltpu.make_async_copy(a, b, small.at[i])
-        for i, (a, b) in enumerate(((x_hbm, x), (src_hbm, src), (dst_hbm, dst)))
+    o = 3 - 2 * own_core()
+    *copies, load = [
+        pltpu.make_async_copy(a, b, sems.at[i])
+        for i, (a, b) in enumerate(((x_hbm, x), (src_hbm, src), (dst_hbm, dst), (tiles_hbm.at[:, o], tiles.at[:, 0])))
     ]
-    o = 3 - 2 * own_core()
-    loads = [
-        pltpu.make_async_copy(tiles_hbm.at[:, p], tiles.at[:, p], large.at[i])
-        for i, p in enumerate((o, 2, 4 - o, 0))
-    ]
-    for c in copies + loads:
+    for c in (*copies, load):
         c.start()
     acc[...] = jnp.zeros_like(acc)
     row = lax.broadcasted_iota(jnp.int32, (width, x.shape[1]), 0)
@@ -124,11 +121,9 @@
         ).astype(BF16)
     for k in range(slots):
         index[k] = src[k] * SRC_UNIT + dst[k]
-    loads[0].wait()
+    load.wait()
     slot_loop(count[0], groups, (o,), functools.partial(push, xt, tiles, index, count[0], acc))
     swap[...] = acc[:blocks].astype(BF16)
-    for c in loads[1:]:
-        c.wait()
 
 
 def forward_send_kernel(count, index, xt, tiles, acc2, direct, acc):
@@ -314,7 +309,7 @@
     piece = jax.ShapeDtypeStruct((blocks, width, BLOCK), BF16)
     totals = jax.ShapeDtypeStruct((blocks + 1, width, BLOCK), F32)
     acc = pltpu.VMEM(totals.shape, F32)
-    tiles = jax.ShapeDtypeStruct((groups, REACH, BLOCK, BLOCK), BF16)
+    tiles = tile_values.reshape(groups, REACH, BLOCK, BLOCK)
     slots = jax.ShapeDtypeStruct((capacity,), jnp.int32)
     rows = jax.ShapeDtypeStruct((nodes, hid), BF16)
     gradient = jax.ShapeDtypeStruct(((f_in + 32) // 2, hid), BF16)
@@ -323,21 +318,21 @@
     def swapped(i):
         return i ^ 1
 
-    tiles, xt, swap, index = call(
+    xt, swap, index = call(
         forward_swap_kernel,
-        [tiles, piece, piece, slots],
+        [piece, piece, slots],
         [SMEM] + [HBM] * 4,
-        [VMEM] * 3 + [SMEM],
+        [VMEM] * 2 + [SMEM],
         [
             pltpu.SMEM((capacity,), jnp.int32),
             pltpu.SMEM((capacity,), jnp.int32),
             pltpu.VMEM(node_features.shape, BF16),
+            pltpu.VMEM((groups, 1, BLOCK, BLOCK), BF16),
             acc,
-            pltpu.SemaphoreType.DMA((3,)),
-            pltpu.SemaphoreType.DMA((REACH,)),
+            pltpu.SemaphoreType.DMA((4,)),
         ],
         flops,
-    )(tile_counts, *(in_hbm(a) for a in (tile_src, tile_dst, node_features, tile_values.reshape(tiles.shape))))
+    )(tile_counts, *(in_hbm(a) for a in (tile_src, tile_dst, node_features, tiles)))
     index = (tile_counts, index)
     swap = moved(swap, "dom", swapped)
     acc2, direct = call(
@@ -350,9 +345,11 @@
     half_rows = jax.ShapeDtypeStruct((nodes // cut, hid), BF16)
     half_columns = jax.ShapeDtypeStruct((f_in + 32, nodes // cut), BF16)
     chip = call(functools.partial(sum_kernel, 2, 0), [half] * cut, [VMEM] * 2, [VMEM] * cut)(acc2, swap)
-    chip = [moved(c, "dom", lambda i: i + 2) for c in chip]
     direct = moved(direct, "dom", lambda i: i + 1 + 2 * (i % 2))
     (acc0,) = call(forward_own_kernel, [totals], [SMEM] * 2 + [VMEM] * 2, [VMEM], (), flops)(*index, xt, tiles)
+    acc0, *later = lax.optimization_barrier((acc0, *chip[1:]))
+    chip = [chip[0], *later]
+    chip = [moved(c, "dom", lambda i: i + 2) for c in chip]
     h_lists = []
     for first, c in zip(starts, chip):
         (h,) = call(functools.partial(sum_kernel, 3, first), [half], [VMEM] * 3, [VMEM])(acc0, direct, c)

time: 40.4 us -> 42.5 us (1.052)
  the two profiles are of different devices: /device:TPU:5 before, /device:TPU:1 now
where the time goes in v1:
time: 42.5 us; the launch traced here: 42.9 us
  starting transfers between devices  20 us (47%)
  Pallas kernels  16 us (38%)
  waiting for transfers between devices  5.26 us (12%)
  between operations  1.61 us (4%)
    ppermute x17, starting transfers between devices, moved(): return lax.ppermute(block, axis, [(i, target(i) % n) for i in range(n)])  20 us
    ppermute x17, waiting for transfers between devices, moved(): return lax.ppermute(block, axis, [(i, target(i) % n) for i in range(n)])  5.26 us
    pallas_call x1, Pallas kernels, shards(): call(forward_swap_kernel, [piece, piece, slots], [SMEM] + [HBM] * 4, [VME...  3.36 us
    pallas_call x1, Pallas kernels, shards(): call(backward_last_kernel, [jax.ShapeDtypeStruct((width, nodes), BF16), j...  2.49 us
    pallas_call x1, Pallas kernels, shards(): call(forward_send_kernel, [totals, piece], [SMEM] * 2 + [VMEM] * 2, [VMEM...  2.38 us
    pallas_call x1, Pallas kernels, shards(): call(backward_near_kernel, [totals, totals], [SMEM] * 2 + [VMEM] * 3, [VM...  1.98 us
    pallas_call x1, Pallas kernels, shards(): call(forward_own_kernel, [totals], [SMEM] * 2 + [VMEM] * 2, [VMEM], (), f...  1.89 us
    pallas_call x2, Pallas kernels, shards(): call(functools.partial(middle_kernel, parts, first), [half_rows, half_col...  1.8 us
  transfers between devices with their start and end apart: 17, of which 3 were waited for; matrix products, arithmetic and copies ran while one was open for 0% of the time, Pallas kernels for 24%

profile of v1, /device:TPU:1, one launch (start us, length us, event | category | flops | bytes accessed | tf_op | source)
XLA Modules:
  0.0 42.9 jit_solution(3885630501717651751)
XLA Ops:
  1.4 3.4 %shard_map.111 = (bf16[8,64,128]{2,1,0:T(8,128)(2,1)S(1)}, bf16[8,64,128]{2,1,0:T(8,128)(2,1)S(1)}, s32[96]{0:T(128)S(1)}) custom-call(s32[1]{0:T(128)S(6)} %copy.12.count, s32[96]{0:T(128)} %src_hbm.1, s32[96]{0:T(128)} %dst_hbm.1, bf16[1024,128]{1,0:T(8,128)(2,1)} %x_hbm.1, bf16[24,4,128,128]{3,2,1,0:T(8,128)(2,1)} %bitcast.4), custom_call_target="tpu_custom_call" | custom-call | flops 50331648 | bytes 1048576 | tf_op jit(solution)/shard_map/pallas_call | solution.py:321
  4.9 2.4 %shard_map.113 = (f32[9,64,128]{2,1,0:T(8,128)S(1)}, bf16[8,64,128]{2,1,0:T(8,128)(2,1)S(1)}) custom-call(s32[1]{0:T(128)S(6)} %copy.12.count, s32[96]{0:T(128)S(1)} %get-tuple-element.39.index, bf16[8,64,128]{2,1,0:T(8,128)(2,1)S(1)} %get-tuple-element.40.xt, bf16[24,4,128,128]{3,2,1,0:T(8,128)(2,1)S(1)} %bitcast.5), custom_call_target="tpu_custom_call" | custom-call | flops 100663296 | bytes 1048576 | tf_op jit(solution)/shard_map/pallas_call | solution.py:338
  7.3 0.8 %collective-permute-start.1 = (bf16[8,64,128]{2,1,0:T(8,128)(2,1)S(1)}, bf16[8,64,128]{2,1,0:T(8,128)(2,1)S(1)}, u32[]{:S(2)}, u32[]{:S(2)}) collective-permute-start(bf16[8,64,128]{2,1,0:T(8,128)(2,1)S(1)} %get-tuple-element.45), channel_id=1, source_target_pairs={{0,2},{2,8},{4,6},{6,12},{8,10},{10,16},{12,14},{14,20},{16,18},{1... | collective-permute-start | bytes 393224 | tf_op jit(solution)/shard_map/ppermute | solution.py:285
  8.1 1.9 %shard_map.112.refs_0_ = f32[9,64,128]{2,1,0:T(8,128)S(1)} custom-call(s32[1]{0:T(128)S(6)} %copy.12.count, s32[96]{0:T(128)S(1)} %get-tuple-element.39.index, bf16[8,64,128]{2,1,0:T(8,128)(2,1)S(1)} %get-tuple-element.40.xt, bf16[24,4,128,128]{3,2,1,0:T(8,128)(2,1)S(1)} %bitcast.6), custom_call_target="tpu_custom_call" | custom-call | flops 50331648 | bytes 1048576 | tf_op jit(solution)/shard_map/pallas_call | solution.py:349
  10.0 1.6 %collective-permute-start.5 = (bf16[4,64,128]{2,1,0:T(8,128)(2,1)S(1)}, bf16[4,64,128]{2,1,0:T(8,128)(2,1)S(1)}, u32[]{:S(2)}, u32[]{:S(2)}) collective-permute-start(bf16[4,64,128]{2,1,0:T(8,128)(2,1)S(1)} %get-tuple-element.49), channel_id=1, source_target_pairs={{0,4},{2,6},{4,8},{6,10},{8,12},{10,14},{12,16},{14,18},{16,20},{1... | collective-permute-start | bytes 196616 | tf_op jit(solution)/shard_map/ppermute | solution.py:285
  11.7 4.3 %collective-permute-done.5.refs_2_ = bf16[4,64,128]{2,1,0:T(8,128)(2,1)S(1)} collective-permute-done((bf16[4,64,128]{2,1,0:T(8,128)(2,1)S(1)}, bf16[4,64,128]{2,1,0:T(8,128)(2,1)S(1)}, u32[]{:S(2)}, u32[]{:S(2)}) %collective-permute-start.5) | collective-permute-done | bytes 65568 | tf_op jit(solution)/shard_map/ppermute | solution.py:285
  16.0 2.2 %collective-permute-start.6 = (bf16[4,64,128]{2,1,0:T(8,128)(2,1)S(1)}, bf16[4,64,128]{2,1,0:T(8,128)(2,1)S(1)}, u32[]{:S(2)}, u32[]{:S(2)}) collective-permute-start(bf16[4,64,128]{2,1,0:T(8,128)(2,1)S(1)} %shard_map.117.refs_0_), channel_id=1, source_target_pairs={{0,1},{1,0},{2,3},{3,2},{4,5},{5,4},{6,7},{7,6},{8,9},{9,8},{10,11... | collective-permute-start | bytes 196616 | tf_op jit(solution)/shard_map/ppermute | solution.py:285
  18.2 1.4 %collective-permute-start.3 = (bf16[4,64,128]{2,1,0:T(8,128)(2,1)S(1)}, bf16[4,64,128]{2,1,0:T(8,128)(2,1)S(1)}, u32[]{:S(2)}, u32[]{:S(2)}) collective-permute-start(bf16[4,64,128]{2,1,0:T(8,128)(2,1)S(1)} %shard_map.115.refs_0_), channel_id=1, source_target_pairs={{0,1},{1,0},{2,3},{3,2},{4,5},{5,4},{6,7},{7,6},{8,9},{9,8},{10,11... | collective-permute-start | bytes 196616 | tf_op jit(solution)/shard_map/ppermute | solution.py:285
  19.6 0.6 %collective-permute-done.6.refs_1_ = bf16[4,64,128]{2,1,0:T(8,128)(2,1)S(1)} collective-permute-done((bf16[4,64,128]{2,1,0:T(8,128)(2,1)S(1)}, bf16[4,64,128]{2,1,0:T(8,128)(2,1)S(1)}, u32[]{:S(2)}, u32[]{:S(2)}) %collective-permute-start.6) | collective-permute-done | bytes 65568 | tf_op jit(solution)/shard_map/ppermute | solution.py:285
  20.2 0.9 %shard_map.118 = (bf16[512,128]{1,0:T(8,128)(2,1)S(1)}, bf16[160,512]{1,0:T(8,128)(2,1)S(1)}, bf16[512,128]{1,0:T(8,128)(2,1)S(1)}, f32[4,64,128]{2,1,0:T(8,128)S(1)}, bf16[4,64,128]{2,1,0:T(8,128)(2,1)S(1)}) custom-call(f32[1,128]{1,0:T(1,128)S(1)} %bitcast.10, bf16[128,128]{1,0:T(8,128)(2,1)S(1)} %copy-done.2, bf16[1024,128]{1,0:T(8,128)(2,1)S(1)} %copy-done.1, ...), custom_call_target="tpu_custom_call" | custom-call | flops 33554432 | bytes 1048576 | tf_op jit(solution)/shard_map/pallas_call | solution.py:359
  21.1 1.1 %collective-permute-start.7 = (bf16[4,64,128]{2,1,0:T(8,128)(2,1)S(1)}, bf16[4,64,128]{2,1,0:T(8,128)(2,1)S(1)}, u32[]{:S(2)}, u32[]{:S(2)}) collective-permute-start(bf16[4,64,128]{2,1,0:T(8,128)(2,1)S(1)} %get-tuple-element.51), channel_id=1, source_target_pairs={{0,1},{1,0},{2,3},{3,2},{4,5},{5,4},{6,7},{7,6},{8,9},{9,8},{10,11... | collective-permute-start | bytes 196616 | tf_op jit(solution)/shard_map/ppermute | solution.py:285
  22.3 0.9 %shard_map.116 = (bf16[512,128]{1,0:T(8,128)(2,1)S(1)}, bf16[160,512]{1,0:T(8,128)(2,1)S(1)}, bf16[512,128]{1,0:T(8,128)(2,1)S(1)}, f32[4,64,128]{2,1,0:T(8,128)S(1)}, bf16[4,64,128]{2,1,0:T(8,128)(2,1)S(1)}) custom-call(f32[1,128]{1,0:T(1,128)S(1)} %bitcast.11, bf16[128,128]{1,0:T(8,128)(2,1)S(1)} %copy-done.2, bf16[1024,128]{1,0:T(8,128)(2,1)S(1)} %copy-done.1, ...), custom_call_target="tpu_custom_call" | custom-call | flops 33554432 | bytes 1048576 | tf_op jit(solution)/shard_map/pallas_call | solution.py:359
  23.2 1.2 %collective-permute-start.4 = (bf16[4,64,128]{2,1,0:T(8,128)(2,1)S(1)}, bf16[4,64,128]{2,1,0:T(8,128)(2,1)S(1)}, u32[]{:S(2)}, u32[]{:S(2)}) collective-permute-start(bf16[4,64,128]{2,1,0:T(8,128)(2,1)S(1)} %get-tuple-element.48), channel_id=1, source_target_pairs={{0,1},{1,0},{2,3},{3,2},{4,5},{5,4},{6,7},{7,6},{8,9},{9,8},{10,11... | collective-permute-start | bytes 196616 | tf_op jit(solution)/shard_map/ppermute | solution.py:285
  24.5 1.3 %collective-permute-start.10 = (bf16[80,128]{1,0:T(8,128)(2,1)S(1)}, bf16[80,128]{1,0:T(8,128)(2,1)S(1)}, u32[]{:S(2)}, u32[]{:S(2)}) collective-permute-start(bf16[80,128]{1,0:T(8,128)(2,1)S(1)} %get-tuple-element.61), channel_id=1, source_target_pairs={{0,2},{2,0},{4,6},{6,4},{8,10},{10,8},{12,14},{14,12},{16,18},{18,... | collective-permute-start | bytes 61448 | tf_op jit(solution)/shard_map/ppermute | solution.py:285
  25.9 1.7 %collective-permute-start.12 = (bf16[80,128]{1,0:T(8,128)(2,1)S(1)}, bf16[80,128]{1,0:T(8,128)(2,1)S(1)}, u32[]{:S(2)}, u32[]{:S(2)}) collective-permute-start(bf16[80,128]{1,0:T(8,128)(2,1)S(1)} %get-tuple-element.61), channel_id=1, source_target_pairs={{0,6},{2,4},{4,2},{6,0},{8,14},{10,12},{12,10},{14,8},{16,22},{18,... | collective-permute-start | bytes 61448 | tf_op jit(solution)/shard_map/ppermute | solution.py:285
  27.6 1.6 %collective-permute-start.8 = (bf16[8,64,128]{2,1,0:T(8,128)(2,1)S(1)}, bf16[8,64,128]{2,1,0:T(8,128)(2,1)S(1)}, u32[]{:S(2)}, u32[]{:S(2)}) collective-permute-start(bf16[8,64,128]{2,1,0:T(8,128)(2,1)S(1)} %shard_map.119.g), channel_id=1, source_target_pairs={{0,28},{2,30},{4,0},{6,2},{8,4},{10,6},{12,8},{14,10},{16,12},{18,... | collective-permute-start | bytes 393224 | tf_op jit(solution)/shard_map/ppermute | solution.py:285
  29.3 1.8 %collective-permute-start.9 = (bf16[8,64,128]{2,1,0:T(8,128)(2,1)S(1)}, bf16[8,64,128]{2,1,0:T(8,128)(2,1)S(1)}, u32[]{:S(2)}, u32[]{:S(2)}) collective-permute-start(bf16[8,64,128]{2,1,0:T(8,128)(2,1)S(1)} %shard_map.119.g), channel_id=1, source_target_pairs={{0,26},{2,0},{4,30},{6,4},{8,2},{10,8},{12,6},{14,12},{16,10},{18,... | collective-permute-start | bytes 393224 | tf_op jit(solution)/shard_map/ppermute | solution.py:285
  31.2 0.9 %collective-permute-start.14 = (bf16[80,128]{1,0:T(8,128)(2,1)S(1)}, bf16[80,128]{1,0:T(8,128)(2,1)S(1)}, u32[]{:S(2)}, u32[]{:S(2)}) collective-permute-start(bf16[80,128]{1,0:T(8,128)(2,1)S(1)} %shard_map.122.refs_0_), channel_id=1, source_target_pairs={{0,16},{2,18},{4,20},{6,22},{8,24},{10,26},{12,28},{14,30},{16,0},... | collective-permute-start | bytes 61448 | tf_op jit(solution)/shard_map/ppermute | solution.py:285
  32.1 2.6 %collective-permute-start.15 = (bf16[80,128]{1,0:T(8,128)(2,1)S(1)}, bf16[80,128]{1,0:T(8,128)(2,1)S(1)}, u32[]{:S(2)}, u32[]{:S(2)}) collective-permute-start(bf16[80,128]{1,0:T(8,128)(2,1)S(1)} %shard_map.122.refs_0_), channel_id=1, source_target_pairs={{0,24},{2,26},{4,28},{6,30},{8,16},{10,18},{12,20},{14,22},{16,8},... | collective-permute-start | bytes 61448 | tf_op jit(solution)/shard_map/ppermute | solution.py:285
  34.7 1.7 %shard_map.120 = (f32[9,64,128]{2,1,0:T(8,128)S(1)}, bf16[1024,128]{1,0:T(8,128)(2,1)}) custom-call(s32[1]{0:T(128)S(6)} %copy.12.count, s32[96]{0:T(128)S(1)} %get-tuple-element.39.index, bf16[24,4,128,128]{3,2,1,0:T(8,128)(2,1)S(1)} %bitcast.7, bf16[8,64,128]{2,1,0:T(8,128)(2,1)S(1)} %shard_map.119.g, bf16[512,128]{1,0:T(8,128)(2,1)S(1)} %get-tuple-element.52.refs_0_, ...), custom_call_target="tpu_custom_call" | custom-call | flops 50331648 | bytes 1048576 | tf_op jit(solution)/shard_map/pallas_call | solution.py:389
  36.4 0.4 collective-permute-done.15.refs_3_
  36.9 1.5 %collective-permute-start.16 = (bf16[592,128]{1,0:T(8,128)(2,1)S(1)}, bf16[592,128]{1,0:T(8,128)(2,1)S(1)}, u32[]{:S(2)}, u32[]{:S(2)}) collective-permute-start(bf16[592,128]{1,0:T(8,128)(2,1)S(1)} %shard_map.123.sent), channel_id=1, source_target_pairs={{0,2},{2,0},{4,6},{6,4},{8,10},{10,8},{12,14},{14,12},{16,18},{18,... | collective-permute-start | bytes 454664 | tf_op jit(solution)/shard_map/ppermute | solution.py:285
  38.4 2.0 %shard_map.124 = (f32[9,64,128]{2,1,0:T(8,128)S(1)}, f32[9,64,128]{2,1,0:T(8,128)S(1)}) custom-call(s32[1]{0:T(128)S(6)} %copy.12.count, s32[96]{0:T(128)S(1)} %get-tuple-element.39.index, bf16[24,4,128,128]{3,2,1,0:T(8,128)(2,1)S(1)} %bitcast.8, bf16[8,64,128]{2,1,0:T(8,128)(2,1)S(1)} %collective-permute-done.8.g.g2, ...), custom_call_target="tpu_custom_call" | custom-call | flops 100663296 | bytes 1048576 | tf_op jit(solution)/shard_map/pallas_call | solution.py:401
  40.4 2.5 %shard_map.125 = (bf16[64,1024]{1,0:T(8,128)(2,1)}, f32[128,128]{1,0:T(8,128)}, f32[1,128]{1,0:T(1,128)}) custom-call(s32[1]{0:T(128)S(6)} %copy.12.count, s32[96]{0:T(128)S(1)} %get-tuple-element.39.index, bf16[24,4,128,128]{3,2,1,0:T(8,128)(2,1)S(1)} %bitcast.9, bf16[592,128]{1,0:T(8,128)(2,1)S(1)} %shard_map.123.sent, ...), custom_call_target="tpu_custom_call" | custom-call | flops 50331648 | bytes 1048576 | tf_op jit(solution)/shard_map/pallas_call | solution.py:404
  (33 shorter events, 0.7 us)
Async XLA Ops:
  0.6 4.3 %copy-start = (bf16[96,128,128]{2,1,0:T(8,128)(2,1)S(1)}, bf16[96,128,128]{2,1,0:T(8,128)(2,1)}, u32[]{:S(2)}) copy-start(bf16[96,128,128]{2,1,0:T(8,128)(2,1)} %param.11) | copy-start | bytes 9437188
  4.8 5.2 %collective-permute-start = (bf16[8,64,128]{2,1,0:T(8,128)(2,1)S(1)}, bf16[8,64,128]{2,1,0:T(8,128)(2,1)S(1)}, u32[]{:S(2)}, u32[]{:S(2)}) collective-permute-start(bf16[8,64,128]{2,1,0:T(8,128)(2,1)S(1)} %get-tuple-element.42), channel_id=1, source_target_pairs={{0,2},{2,0},{4,6},{6,4},{8,10},{10,8},{12,14},{14,12},{16,18},{18,... | collective-permute-start | bytes 393224 | tf_op jit(solution)/shard_map/ppermute | solution.py:285
  7.3 12.9 %copy-start.1 = (bf16[1024,128]{1,0:T(8,128)(2,1)S(1)}, bf16[1024,128]{1,0:T(8,128)(2,1)}, u32[]{:S(2)}) copy-start(bf16[1024,128]{1,0:T(8,128)(2,1)} %og_ref.3) | copy-start | bytes 786436
  7.3 12.9 %copy-start.2 = (bf16[128,128]{1,0:T(8,128)(2,1)S(1)}, bf16[128,128]{1,0:T(8,128)(2,1)}, u32[]{:S(2)}) copy-start(bf16[128,128]{1,0:T(8,128)(2,1)} %w_ref.3) | copy-start | bytes 98308
  7.3 12.9 %copy-start.3 = (f32[128]{0:T(128)S(1)}, f32[128]{0:T(128)}, u32[]{:S(2)}) copy-start(f32[128]{0:T(128)} %param.10) | copy-start | bytes 1540
  7.3 4.4 %collective-permute-start.1 = (bf16[8,64,128]{2,1,0:T(8,128)(2,1)S(1)}, bf16[8,64,128]{2,1,0:T(8,128)(2,1)S(1)}, u32[]{:S(2)}, u32[]{:S(2)}) collective-permute-start(bf16[8,64,128]{2,1,0:T(8,128)(2,1)S(1)} %get-tuple-element.45), channel_id=1, source_target_pairs={{0,2},{2,8},{4,6},{6,12},{8,10},{10,16},{12,14},{14,20},{16,18},{1... | collective-permute-start | bytes 393224 | tf_op jit(solution)/shard_map/ppermute | solution.py:285
  10.0 6.0 %collective-permute-start.5 = (bf16[4,64,128]{2,1,0:T(8,128)(2,1)S(1)}, bf16[4,64,128]{2,1,0:T(8,128)(2,1)S(1)}, u32[]{:S(2)}, u32[]{:S(2)}) collective-permute-start(bf16[4,64,128]{2,1,0:T(8,128)(2,1)S(1)} %get-tuple-element.49), channel_id=1, source_target_pairs={{0,4},{2,6},{4,8},{6,10},{8,12},{10,14},{12,16},{14,18},{16,20},{1... | collective-permute-start | bytes 196616 | tf_op jit(solution)/shard_map/ppermute | solution.py:285
  11.6 6.6 %collective-permute-start.2 = (bf16[4,64,128]{2,1,0:T(8,128)(2,1)S(1)}, bf16[4,64,128]{2,1,0:T(8,128)(2,1)S(1)}, u32[]{:S(2)}, u32[]{:S(2)}) collective-permute-start(bf16[4,64,128]{2,1,0:T(8,128)(2,1)S(1)} %get-tuple-element.46), channel_id=1, source_target_pairs={{0,4},{2,6},{4,8},{6,10},{8,12},{10,14},{12,16},{14,18},{16,20},{1... | collective-permute-start | bytes 196616 | tf_op jit(solution)/shard_map/ppermute | solution.py:285
  16.0 4.2 %collective-permute-start.6 = (bf16[4,64,128]{2,1,0:T(8,128)(2,1)S(1)}, bf16[4,64,128]{2,1,0:T(8,128)(2,1)S(1)}, u32[]{:S(2)}, u32[]{:S(2)}) collective-permute-start(bf16[4,64,128]{2,1,0:T(8,128)(2,1)S(1)} %shard_map.117.refs_0_), channel_id=1, source_target_pairs={{0,1},{1,0},{2,3},{3,2},{4,5},{5,4},{6,7},{7,6},{8,9},{9,8},{10,11... | collective-permute-start | bytes 196616 | tf_op jit(solution)/shard_map/ppermute | solution.py:285
  18.2 4.0 %collective-permute-start.3 = (bf16[4,64,128]{2,1,0:T(8,128)(2,1)S(1)}, bf16[4,64,128]{2,1,0:T(8,128)(2,1)S(1)}, u32[]{:S(2)}, u32[]{:S(2)}) collective-permute-start(bf16[4,64,128]{2,1,0:T(8,128)(2,1)S(1)} %shard_map.115.refs_0_), channel_id=1, source_target_pairs={{0,1},{1,0},{2,3},{3,2},{4,5},{5,4},{6,7},{7,6},{8,9},{9,8},{10,11... | collective-permute-start | bytes 196616 | tf_op jit(solution)/shard_map/ppermute | solution.py:285
  21.1 6.5 %collective-permute-start.7 = (bf16[4,64,128]{2,1,0:T(8,128)(2,1)S(1)}, bf16[4,64,128]{2,1,0:T(8,128)(2,1)S(1)}, u32[]{:S(2)}, u32[]{:S(2)}) collective-permute-start(bf16[4,64,128]{2,1,0:T(8,128)(2,1)S(1)} %get-tuple-element.51), channel_id=1, source_target_pairs={{0,1},{1,0},{2,3},{3,2},{4,5},{5,4},{6,7},{7,6},{8,9},{9,8},{10,11... | collective-permute-start | bytes 196616 | tf_op jit(solution)/shard_map/ppermute | solution.py:285
  23.2 4.5 %collective-permute-start.4 = (bf16[4,64,128]{2,1,0:T(8,128)(2,1)S(1)}, bf16[4,64,128]{2,1,0:T(8,128)(2,1)S(1)}, u32[]{:S(2)}, u32[]{:S(2)}) collective-permute-start(bf16[4,64,128]{2,1,0:T(8,128)(2,1)S(1)} %get-tuple-element.48), channel_id=1, source_target_pairs={{0,1},{1,0},{2,3},{3,2},{4,5},{5,4},{6,7},{7,6},{8,9},{9,8},{10,11... | collective-permute-start | bytes 196616 | tf_op jit(solution)/shard_map/ppermute | solution.py:285
  24.5 6.5 %collective-permute-start.10 = (bf16[80,128]{1,0:T(8,128)(2,1)S(1)}, bf16[80,128]{1,0:T(8,128)(2,1)S(1)}, u32[]{:S(2)}, u32[]{:S(2)}) collective-permute-start(bf16[80,128]{1,0:T(8,128)(2,1)S(1)} %get-tuple-element.61), channel_id=1, source_target_pairs={{0,2},{2,0},{4,6},{6,4},{8,10},{10,8},{12,14},{14,12},{16,18},{18,... | collective-permute-start | bytes 61448 | tf_op jit(solution)/shard_map/ppermute | solution.py:285
  25.9 5.2 %collective-permute-start.11 = (bf16[80,128]{1,0:T(8,128)(2,1)S(1)}, bf16[80,128]{1,0:T(8,128)(2,1)S(1)}, u32[]{:S(2)}, u32[]{:S(2)}) collective-permute-start(bf16[80,128]{1,0:T(8,128)(2,1)S(1)} %get-tuple-element.60.refs_0_), channel_id=1, source_target_pairs={{0,4},{2,6},{4,0},{6,2},{8,12},{10,14},{12,8},{14,10},{16,20},{18,... | collective-permute-start | bytes 61448 | tf_op jit(solution)/shard_map/ppermute | solution.py:285
  25.9 5.2 %collective-permute-start.12 = (bf16[80,128]{1,0:T(8,128)(2,1)S(1)}, bf16[80,128]{1,0:T(8,128)(2,1)S(1)}, u32[]{:S(2)}, u32[]{:S(2)}) collective-permute-start(bf16[80,128]{1,0:T(8,128)(2,1)S(1)} %get-tuple-element.61), channel_id=1, source_target_pairs={{0,6},{2,4},{4,2},{6,0},{8,14},{10,12},{12,10},{14,8},{16,22},{18,... | collective-permute-start | bytes 61448 | tf_op jit(solution)/shard_map/ppermute | solution.py:285
  27.6 9.2 %collective-permute-start.8 = (bf16[8,64,128]{2,1,0:T(8,128)(2,1)S(1)}, bf16[8,64,128]{2,1,0:T(8,128)(2,1)S(1)}, u32[]{:S(2)}, u32[]{:S(2)}) collective-permute-start(bf16[8,64,128]{2,1,0:T(8,128)(2,1)S(1)} %shard_map.119.g), channel_id=1, source_target_pairs={{0,28},{2,30},{4,0},{6,2},{8,4},{10,6},{12,8},{14,10},{16,12},{18,... | collective-permute-start | bytes 393224 | tf_op jit(solution)/shard_map/ppermute | solution.py:285
  29.3 7.6 %collective-permute-start.9 = (bf16[8,64,128]{2,1,0:T(8,128)(2,1)S(1)}, bf16[8,64,128]{2,1,0:T(8,128)(2,1)S(1)}, u32[]{:S(2)}, u32[]{:S(2)}) collective-permute-start(bf16[8,64,128]{2,1,0:T(8,128)(2,1)S(1)} %shard_map.119.g), channel_id=1, source_target_pairs={{0,26},{2,0},{4,30},{6,4},{8,2},{10,8},{12,6},{14,12},{16,10},{18,... | collective-permute-start | bytes 393224 | tf_op jit(solution)/shard_map/ppermute | solution.py:285
  31.1 5.3 %collective-permute-start.13 = (bf16[80,128]{1,0:T(8,128)(2,1)S(1)}, bf16[80,128]{1,0:T(8,128)(2,1)S(1)}, u32[]{:S(2)}, u32[]{:S(2)}) collective-permute-start(bf16[80,128]{1,0:T(8,128)(2,1)S(1)} %shard_map.122.refs_0_), channel_id=1, source_target_pairs={{0,8},{2,10},{4,12},{6,14},{8,0},{10,2},{12,4},{14,6},{16,24},{18,... | collective-permute-start | bytes 61448 | tf_op jit(solution)/shard_map/ppermute | solution.py:285
  31.2 5.3 %collective-permute-start.14 = (bf16[80,128]{1,0:T(8,128)(2,1)S(1)}, bf16[80,128]{1,0:T(8,128)(2,1)S(1)}, u32[]{:S(2)}, u32[]{:S(2)}) collective-permute-start(bf16[80,128]{1,0:T(8,128)(2,1)S(1)} %shard_map.122.refs_0_), channel_id=1, source_target_pairs={{0,16},{2,18},{4,20},{6,22},{8,24},{10,26},{12,28},{14,30},{16,0},... | collective-permute-start | bytes 61448 | tf_op jit(solution)/shard_map/ppermute | solution.py:285
  32.1 4.7 %collective-permute-start.15 = (bf16[80,128]{1,0:T(8,128)(2,1)S(1)}, bf16[80,128]{1,0:T(8,128)(2,1)S(1)}, u32[]{:S(2)}, u32[]{:S(2)}) collective-permute-start(bf16[80,128]{1,0:T(8,128)(2,1)S(1)} %shard_map.122.refs_0_), channel_id=1, source_target_pairs={{0,24},{2,26},{4,28},{6,30},{8,16},{10,18},{12,20},{14,22},{16,8},... | collective-permute-start | bytes 61448 | tf_op jit(solution)/shard_map/ppermute | solution.py:285
  36.9 3.5 %collective-permute-start.16 = (bf16[592,128]{1,0:T(8,128)(2,1)S(1)}, bf16[592,128]{1,0:T(8,128)(2,1)S(1)}, u32[]{:S(2)}, u32[]{:S(2)}) collective-permute-start(bf16[592,128]{1,0:T(8,128)(2,1)S(1)} %shard_map.123.sent), channel_id=1, source_target_pairs={{0,2},{2,0},{4,6},{6,4},{8,10},{10,8},{12,14},{14,12},{16,18},{18,... | collective-permute-start | bytes 454664 | tf_op jit(solution)/shard_map/ppermute | solution.py:285
